TPU v7x, 32 devices: a whole 2x2x4 slice. The times are simulated.
32 devices in a mesh: row: 4 (over y, x), col: 8 (over z, core).
Axes of the slice: x: 2, y: 2, z: 4, core: 2. Of those that a mesh axis runs over, the one named last changes fastest.
Arguments:
- trailing: float32 [10, 4, 256, 5, 8, 256], P(None, 'row', None, None, 'col'), as said below
Outputs:
- factored: float32 [10, 4, 256, 5, 8, 256], P(None, 'row', None, None, 'col')
Inputs may be any that keep to these rules, and one draw needn't show every extreme that they name: trailing is a covariance matrix of points in the plane: symmetric and positive definite, with a nugget added to its diagonal.
All inputs are finite; a program needn't handle non-finite values.
Results may differ from a plain program's by a relative error of at most 0.0041.
Values may be sent and summed in bfloat16 or wider, within the bound.
A program may use at most 128 MiB of HBM per device.

v0:
```python
import jax
import jax.numpy as jnp
from jax import lax
from jax.sharding import PartitionSpec as P

PANELS = 2


def broadcast(x, axis, root):
    mine = lax.axis_index(axis) == root
    return lax.psum(jnp.where(mine, x, jnp.zeros_like(x)), axis)


def local_update(panel_rows, partner):
    return lax.dot_general(
        panel_rows, partner, (((1,), (1,)), ((), ())), preferred_element_type=jnp.float32
    )


def factor_panel(blocks, step, row_here, col_here):
    row_blocks, width, col_blocks, _ = blocks.shape
    n_row = lax.axis_size("row")
    n_col = lax.axis_size("col")
    owner_block = blocks[step // n_row, :, step // n_col, :]
    diagonal = broadcast(owner_block, "row", step % n_row)
    settled = jnp.where(col_here == step % n_col, diagonal, jnp.eye(width, dtype=jnp.float32))
    lower = jnp.linalg.cholesky(settled)
    column = blocks[:, :, step // n_col, :].reshape(row_blocks * width, width)
    solved = jax.scipy.linalg.solve_triangular(lower, column.T, lower=True).T.reshape(
        row_blocks, width, width
    )
    global_rows = jnp.arange(row_blocks) * n_row + row_here
    below = (global_rows > step)[:, None, None]
    at_diagonal = (global_rows == step)[:, None, None]
    factor_col = jnp.where(below, solved, jnp.where(at_diagonal, lower[None], 0.0))
    shipped = jnp.where(below, solved, 0.0).astype(jnp.bfloat16).reshape(row_blocks * width, width)
    panel_rows = broadcast(shipped, "col", step % n_col)
    ratio = n_col // n_row
    offset = col_here // n_row
    everything = lax.all_gather(panel_rows, "row", axis=0, tiled=True)
    holder = lax.dynamic_index_in_dim(
        everything.reshape(n_row, row_blocks * width, width), col_here % n_row, 0, keepdims=False
    )
    partner = lax.dynamic_index_in_dim(
        holder.reshape(col_blocks, ratio, width, width), offset, 1, keepdims=False
    )
    return (factor_col, panel_rows, partner.reshape(col_blocks * width, width))


def settle(blocks, step, factor_col, row_here, col_here):
    row_blocks, width, col_blocks, _ = blocks.shape
    n_row = lax.axis_size("row")
    n_col = lax.axis_size("col")
    target = step // n_col
    present = blocks[:, :, target, :]
    blocks = blocks.at[:, :, target, :].set(
        jnp.where(col_here == step % n_col, factor_col, present)
    )
    global_rows = jnp.arange(row_blocks) * n_row + row_here
    global_cols = jnp.arange(col_blocks) * n_col + col_here
    vanish = (global_rows <= step)[:, None, None, None] & (global_cols > step)[None, None, :, None]
    return jnp.where(vanish, 0.0, blocks)


def body(trailing):
    shape_given = trailing.shape
    row_blocks = shape_given[0]
    width = shape_given[2]
    col_blocks = shape_given[3]
    blocks = trailing.reshape(row_blocks, width, col_blocks, width)
    row_here = lax.axis_index("row")
    col_here = lax.axis_index("col")
    current = factor_panel(blocks, 0, row_here, col_here)
    for step in range(PANELS):
        factor_col, panel_rows, partner = current
        whole = local_update(panel_rows, partner).reshape(row_blocks, width, col_blocks, width)
        blocks = blocks - whole
        blocks = settle(blocks, step, factor_col, row_here, col_here)
        if step + 1 < PANELS:
            current = factor_panel(blocks, step + 1, row_here, col_here)
    return blocks.reshape(shape_given)


def solution(mesh):
    placed = (P(None, "row", None, None, "col", None),)
    return jax.shard_map(
        body,
        mesh=mesh,
        in_specs=placed,
        out_specs=P(None, "row", None, None, "col", None),
        check_vma=False,
    )
```

profile of v0, /device:TPU:0, one launch (start us, length us, event | category | flops | bytes accessed | tf_op | source)
XLA Modules:
  0.0 617.2 jit_solution(9852320332539554087)
XLA Ops:
  6.5 27.0 %copy.12 = f32[10,1,256,5,1,256]{2,5,3,0,4,1:T(8,128)} copy(f32[10,1,256,5,1,256]{5,4,3,2,1,0:T(1,128)} %param.8) | data formatting | bytes 26214400 | tf_op args[0]
  33.6 1.7 fusion.13
  35.4 2.0 slice.121
  37.4 2.1 copy.14
  39.6 41.5 %all-reduce.6.cloned.1.call-done = f32[256,256]{0,1:T(8,128)} async-done(((f32[256,256]{0,1:T(8,128)}), f32[256,256]{0,1:T(8,128)}) %all-reduce.6.cloned.1.call-update) | async-done | bytes 262160 | tf_op jit(solution)/shard_map/psum | solution.py:11
  81.1 1.0 convert_select_fusion.1
  82.2 1.0 fusion.15
  83.2 11.7 %cholesky.130 = f32[128,128]{1,0:T(8,128)S(1)} custom-call(f32[128,128]{1,0:T(8,128)S(1)} %cholesky.194), custom_call_target="Cholesky" | custom-call | tf_op jit(solution)/shard_map/jit(cholesky)/cholesky | solution.py:27
  95.0 9.8 %custom-call.13 = f32[1,128,128]{1,2,0:T(8,128)S(1)} custom-call(f32[1,128,128]{2,1,0:T(8,128)S(1)} %get-tuple-element.78), custom_call_target="InvertDiagBlocksLowerTriangular" | custom-call | tf_op jit(solution)/shard_map/jit(cholesky)/cholesky | solution.py:27
  105.3 11.7 %cholesky.147 = f32[128,128]{1,0:T(8,128)S(1)} custom-call(f32[128,128]{1,0:T(8,128)S(1)} %convolution_subtract_fusion.5), custom_call_target="Cholesky" | custom-call | tf_op jit(solution)/shard_map/jit(cholesky)/cholesky | solution.py:27
  117.1 0.7 compare_reduce_fusion.2
  119.1 3.9 while.6
  119.2 0.6 fusion.48
  119.7 1.3 bitcast_dynamic-update-slice_fusion.4
  121.1 0.6 fusion.48
  121.7 1.3 bitcast_dynamic-update-slice_fusion.4
  123.0 20.1 %custom-call.14 = f32[2,128,128]{1,2,0:T(8,128)S(1)} custom-call(f32[2,128,128]{2,1,0:T(8,128)S(1)} %get-tuple-element.45), custom_call_target="InvertDiagBlocksLowerTriangular" | custom-call | tf_op jit(solution)/shard_map/jit(_solve_triangular)/triangular_solve | solution.py:29
  143.1 2.6 fusion.6
  145.7 3.5 convolution_subtract_fusion.3
  149.3 1.3 fusion.24
  150.6 1.3 fusion.2
  152.0 58.3 %all-reduce.8.cloned.1.call-done = bf16[2560,256]{0,1:T(8,128)(2,1)} async-done(((bf16[2560,256]{0,1:T(8,128)(2,1)}), bf16[2560,256]{0,1:T(8,128)(2,1)}) %all-reduce.8.cloned.1.call-update) | async-done | bytes 1310736 | tf_op jit(solution)/shard_map/psum | solution.py:11
  210.5 1.7 maximum_bitcast_fusion
  212.2 3.3 copy.18
  215.4 2.1 copy.20
  217.7 2.6 copy.15
  220.3 52.3 %all-gather.3.cloned.1.call-done = bf16[10240,256]{0,1:T(8,128)(2,1)} async-done(((bf16[2560,256]{0,1:T(8,128)(2,1)}), bf16[10240,256]{0,1:T(8,128)(2,1)}) %all-gather.3.cloned.1.call-update) | async-done | bytes 5242896 | tf_op jit(solution)/shard_map/all_gather | solution.py:40
  272.7 7.9 %copy.34 = bf16[10240,256]{1,0:T(8,128)(2,1)} copy(bf16[10240,256]{0,1:T(8,128)(2,1)} %all-gather.3.cloned.1.call-done) | data formatting | bytes 10485760 | tf_op jit(solution)/shard_map/reshape | solution.py:42
  280.6 1.5 constant_dynamic-slice_fusion.3
  282.3 11.6 %convolution_subtract_fusion.1 = f32[10,256,5,256]{1,3,2,0:T(8,128)} fusion(bf16[10,256,256,1]{2,1,3,0:T(8,128)(2,1)S(1)} %bitcast.121, bf16[5,2,256,256]{3,2,1,0:T(8,128)(2,1)S(1)} %bitcast.123, s32[]{:T(128)S(6)} %select_n.150, f32[10,1,256,5,1,256]{2,5,3,0,4,1:T(8,128)} %copy.12), kind=kOutput, calls=%fused_computation.6 | convolution fusion | flops 1680998400 | bytes 28180484 | tf_op jit(solution)/shard_map/dot_general | solution.py:15
  293.8 3.7 fusion.1
  297.5 12.2 %broadcast_select_fusion = f32[10,256,5,256]{1,3,2,0:T(8,128)} fusion(f32[10,256,5,256]{1,3,2,0:T(8,128)} %fusion.1, pred[10,5]{1,0:T(8,128)(4,1)S(1)} %broadcast_and_fusion), kind=kLoop, calls=%fused_computation.7 | loop fusion | flops 3276800 | bytes 26214450 | tf_op jit(solution)/shard_map/jit(_where)/select_n | solution.py:62
  309.8 1.7 fusion.12
  311.6 1.7 slice-done
  313.4 2.3 copy.22
  315.6 38.9 %all-reduce.10.cloned.1.call-done = f32[256,256]{0,1:T(8,128)} async-done(((f32[256,256]{0,1:T(8,128)}), f32[256,256]{0,1:T(8,128)}) %all-reduce.10.cloned.1.call-update) | async-done | bytes 262160 | tf_op jit(solution)/shard_map/psum | solution.py:11
  354.8 11.7 %cholesky.164 = f32[128,128]{1,0:T(8,128)S(1)} custom-call(f32[128,128]{1,0:T(8,128)S(1)} %cholesky.197), custom_call_target="Cholesky" | custom-call | tf_op jit(solution)/shard_map/jit(cholesky)/cholesky | solution.py:27
  366.6 9.8 %custom-call.15 = f32[1,128,128]{1,2,0:T(8,128)S(1)} custom-call(f32[1,128,128]{2,1,0:T(8,128)S(1)} %get-tuple-element.74), custom_call_target="InvertDiagBlocksLowerTriangular" | custom-call | tf_op jit(solution)/shard_map/jit(cholesky)/cholesky | solution.py:27
  376.6 0.3 convolution_subtract_fusion.4
  376.9 11.7 %cholesky.181 = f32[128,128]{1,0:T(8,128)S(1)} custom-call(f32[128,128]{1,0:T(8,128)S(1)} %convolution_subtract_fusion.4), custom_call_target="Cholesky" | custom-call | tf_op jit(solution)/shard_map/jit(cholesky)/cholesky | solution.py:27
  388.6 0.7 compare_reduce_fusion
  389.3 0.6 compare_reduce_fusion.1
  391.2 3.9 while.7
  391.3 0.6 fusion.49
  391.8 1.3 bitcast_dynamic-update-slice_fusion.5
  393.2 0.6 fusion.49
  393.8 1.3 bitcast_dynamic-update-slice_fusion.5
  395.1 19.9 %custom-call.16 = f32[2,128,128]{1,2,0:T(8,128)S(1)} custom-call(f32[2,128,128]{2,1,0:T(8,128)S(1)} %get-tuple-element.46), custom_call_target="InvertDiagBlocksLowerTriangular" | custom-call | tf_op jit(solution)/shard_map/jit(_solve_triangular)/triangular_solve | solution.py:29
  415.0 2.6 fusion.4
  417.6 3.5 convolution_subtract_fusion.2
  421.1 1.3 fusion.20
  422.4 1.3 fusion.3
  423.8 60.1 %all-reduce.12.cloned.1.call-done = bf16[2560,256]{0,1:T(8,128)(2,1)} async-done(((bf16[2560,256]{0,1:T(8,128)(2,1)}), bf16[2560,256]{0,1:T(8,128)(2,1)}) %all-reduce.12.cloned.1.call-update) | async-done | bytes 1310736 | tf_op jit(solution)/shard_map/psum | solution.py:11
  484.1 1.7 maximum_bitcast_fusion.1
  485.8 3.5 copy.26
  489.3 2.2 copy.28
  491.6 2.6 copy.23
  494.2 51.9 %all-gather.5.cloned.1.call-done = bf16[10240,256]{0,1:T(8,128)(2,1)} async-done(((bf16[2560,256]{0,1:T(8,128)(2,1)}), bf16[10240,256]{0,1:T(8,128)(2,1)}) %all-gather.5.cloned.1.call-update) | async-done | bytes 5242896 | tf_op jit(solution)/shard_map/all_gather | solution.py:40
  546.1 7.9 %copy.35 = bf16[10240,256]{1,0:T(8,128)(2,1)} copy(bf16[10240,256]{0,1:T(8,128)(2,1)} %all-gather.5.cloned.1.call-done) | data formatting | bytes 10485760 | tf_op jit(solution)/shard_map/reshape | solution.py:42
  554.0 1.5 constant_dynamic-slice_fusion.2
  555.7 11.6 %convolution_subtract_fusion = f32[10,256,5,256]{1,3,2,0:T(8,128)} fusion(f32[10,256,5,256]{1,3,2,0:T(8,128)} %broadcast_select_fusion, bf16[10,256,256,1]{2,1,3,0:T(8,128)(2,1)S(1)} %bitcast.120, bf16[5,2,256,256]{3,2,1,0:T(8,128)(2,1)S(1)} %bitcast.122, s32[]{:T(128)S(6)} %select_n.150), kind=kOutput, calls=%fused_computation.5 | convolution fusion | flops 1680998400 | bytes 28180484 | tf_op jit(solution)/shard_map/dot_general | solution.py:15
  567.3 3.7 fusion
  570.9 12.0 %select_bitcast_fusion = f32[10,1,256,5,1,256]{2,5,3,0,4,1:T(8,128)} fusion(f32[10,256,5,256]{1,3,2,0:T(8,128)} %fusion, pred[10,5]{1,0:T(8,128)(4,1)S(1)} %broadcast_and_fusion.1), kind=kLoop, calls=%fused_computation.4 | loop fusion | flops 3276800 | bytes 26214450 | tf_op jit(solution)/shard_map/reshape | solution.py:81
  582.9 27.2 %copy.29 = f32[10,1,256,5,1,256]{5,4,3,2,1,0:T(1,128)} copy(f32[10,1,256,5,1,256]{2,5,3,0,4,1:T(8,128)} %select_bitcast_fusion) | data formatting | bytes 26214400 | tf_op jit(solution)/shard_map/reshape | solution.py:81
  (56 shorter events, 2.8 us)
Async XLA Ops:
  6.5 74.6 %all-reduce.6.cloned.1.call-start = ((), (), s32[]{:S(2)}) async-start(), calls=%async_computation | async-start | bytes 524288 | tf_op jit(solution)/shard_map/psum | solution.py:11
  35.3 174.9 %all-reduce.8.cloned.1.call-start = ((), (), s32[]{:S(2)}) async-start(), calls=%async_computation.1 | async-start | bytes 2621440 | tf_op jit(solution)/shard_map/psum | solution.py:11
  151.9 120.7 %all-gather.3.cloned.1.call-start = ((), (), s32[]{:S(2)}) async-start(), calls=%async_computation.2 | async-start | bytes 6553600 | tf_op jit(solution)/shard_map/all_gather | solution.py:40
  210.3 144.3 %all-reduce.10.cloned.1.call-start = ((), (), s32[]{:S(2)}) async-start(), calls=%async_computation.3 | async-start | bytes 524288 | tf_op jit(solution)/shard_map/psum | solution.py:11
  280.6 1.7 copy-start.1
  311.5 172.5 %all-reduce.12.cloned.1.call-start = ((), (), s32[]{:S(2)}) async-start(), calls=%async_computation.4 | async-start | bytes 2621440 | tf_op jit(solution)/shard_map/psum | solution.py:11
  311.6 1.7 slice-start
  423.8 122.3 %all-gather.5.cloned.1.call-start = ((), (), s32[]{:S(2)}) async-start(), calls=%async_computation.5 | async-start | bytes 6553600 | tf_op jit(solution)/shard_map/all_gather | solution.py:40
  554.0 1.7 copy-start
Sparse Core Ops, SparseCore 0:
  35.4 45.6 all-reduce.5
  152.0 58.1 all-reduce.7
  212.2 60.3 all-gather.2
  311.6 42.9 all-reduce.9
  423.9 60.0 all-reduce.11
  485.7 60.3 all-gather.4
where the time goes:
time: 628 us; the launch traced here: 617 us
  waiting for transfers between devices  303 us (48%)
  other arithmetic  152 us (24%)
  local copies, waits for them, and re-layouts  106 us (17%)
  matrix products  38.9 us (6%)
  between operations  16.6 us (3%)
    psum x4, waiting for transfers between devices, broadcast(): return lax.psum(jnp.where(mine, x, jnp.zeros_like(x)), axis)  199 us
    all_gather x2, waiting for transfers between devices, factor_panel(): everything = lax.all_gather(panel_rows, 'row', axis=0, tiled=True)  104 us
    another operation x13, other arithmetic, factor_panel(): lower = jnp.linalg.cholesky(settled)  68.6 us
    another operation x5, other arithmetic, factor_panel(): jax.scipy.linalg.solve_triangular(lower, column.T, lower=True)  40.1 us
    unnamed x5, local copies, waits for them, and re-layouts  27.5 us
    reshape x1, local copies, waits for them, and re-layouts, body(): return blocks.reshape(shape_given)  27.2 us
    dot_general x2, matrix products, local_update(): lax.dot_general(panel_rows, partner, (((1,), (1,)), ((), ())), preferred_...  23.2 us
    reshape x2, local copies, waits for them, and re-layouts, factor_panel(): everything.reshape(n_row, row_blocks * width, width)  15.8 us
  transfers between devices with their start and end apart: 6, of which 6 were waited for; matrix products, arithmetic and copies ran while one was open for 4% of the time, Pallas kernels for 0%

commit v1 on v0

v1 whole, which is shorter than its diff:
```python
import functools

import jax
import jax.numpy as jnp
from jax import lax
from jax.experimental import pallas as pl
from jax.experimental.pallas import tpu as pltpu
from jax.sharding import PartitionSpec as P

MESH = pl.DeviceIdType.MESH
HIGHEST = lax.Precision.HIGHEST
OUTER = 64
STRIP = 8
CHUNKS = 4


def dot(a, b, dims, precision=None):
    return lax.dot_general(
        a, b, (dims, ((), ())), precision=precision, preferred_element_type=jnp.float32
    )


def eliminate_block(work, start, width):
    tile = (start // 128) * 128

    def strip(s, carry):
        j0 = pl.multiple_of(start + s * STRIP, STRIP)
        rows = work[pl.ds(j0, STRIP), :]
        near = rows[:, tile:tile + 128]
        lane = lax.broadcasted_iota(jnp.int32, (STRIP, 128), 1) + tile
        sub = lax.broadcasted_iota(jnp.int32, (STRIP, 1), 0)
        cols = [
            jnp.sum(jnp.where(lane == j0 + k, near, 0.0), axis=1, keepdims=True)
            for k in range(STRIP)
        ]
        for k in range(STRIP):
            pivot = cols[k][k:k + 1]
            inv = lax.rsqrt(pivot)
            inv = inv * (1.5 - 0.5 * pivot * inv * inv)
            mult = cols[k] * inv
            for m in range(k + 1, STRIP):
                cols[m] = cols[m] - mult * mult[m:m + 1]
            row = rows[k:k + 1] * inv
            rows = jnp.where(sub == k, row, jnp.where(sub > k, rows - mult * row, rows))
        work[pl.ds(j0, STRIP), :] = rows
        here = lax.broadcasted_iota(jnp.int32, (STRIP, OUTER), 1)
        left = jnp.where(here >= (s + 1) * STRIP, rows[:, start:start + OUTER], 0.0)
        work[start:start + OUTER, :] -= dot(left, rows, ((0,), (0,)), HIGHEST)
        return carry

    lax.fori_loop(0, OUTER // STRIP, strip, 0)
    stop = start + OUTER
    if stop < width:
        done = work[start:stop, :]
        work[stop:width, :] -= dot(done[:, stop:width], done, ((0,), (0,)), HIGHEST)


def load_work(work, block, width):
    work[:, :width] = block
    r = lax.broadcasted_iota(jnp.int32, (width, width), 0)
    c = lax.broadcasted_iota(jnp.int32, (width, width), 1)
    work[:, width:] = jnp.where(r == c, 1.0, 0.0)


def panel_kernel(n_row, n_col, width, col_blocks, local, x_out, u_out, b01_out, bcol, brow,
                 strips, diag, work, local_sem, d_send, d_recv, d_csend, s_send, s_recv,
                 b_send, b_recv):
    r = lax.axis_index("row")
    c = lax.axis_index("col")
    n_z = n_col // 2
    z = c // 2
    core = lax.rem(c, 2)
    ratio = n_col // n_row
    tiles = col_blocks * width // 128
    per = width // 128
    strip_rows = width * tiles

    barrier = pltpu.get_barrier_semaphore()
    for step in range(1, n_row):
        pl.semaphore_signal(barrier, inc=1, device_id=(lax.rem(r + step, n_row), c),
                            device_id_type=MESH)
    pl.semaphore_signal(barrier, inc=1, device_id=(r, z * 2 + 1 - core), device_id_type=MESH)

    @pl.when(z < n_z - 1)
    def _():
        pl.semaphore_signal(barrier, inc=1, device_id=(r, c + 2), device_id_type=MESH)

    @pl.when(z > 0)
    def _():
        pl.semaphore_signal(barrier, inc=1, device_id=(r, c - 2), device_id_type=MESH)

    own = pltpu.make_async_copy(local.at[pl.ds(0, strip_rows)], strips.at[lax.rem(r, 2)],
                                local_sem)

    @pl.when(r < 2)
    def _():
        own.start()

    pl.semaphore_wait(barrier, n_row + jnp.where(z < n_z - 1, 1, 0) + jnp.where(z > 0, 1, 0))

    @pl.when(r < 2)
    def _():
        own.wait()

    owners = ((0, 0), (0, 1), (1, 1))

    def diag_copy(x, step):
        return pltpu.make_async_remote_copy(
            src_ref=diag.at[x], dst_ref=diag.at[x], send_sem=d_send.at[x, step - 1],
            recv_sem=d_recv.at[x], device_id=(lax.rem(r + step, n_row), c), device_id_type=MESH)

    for x, (k, cc) in enumerate(owners):
        @pl.when((r == k) & (c == cc))
        def _(x=x, k=k):
            for h in range(per):
                diag[x, :, h * 128:(h + 1) * 128] = strips[k, pl.ds(h, width, stride=tiles), :]
            for step in range(1, n_row):
                diag_copy(x, step).start()

    def strip_copy(k, step):
        return pltpu.make_async_remote_copy(
            src_ref=strips.at[k], dst_ref=strips.at[k], send_sem=s_send.at[k, step - 1],
            recv_sem=s_recv.at[k], device_id=(lax.rem(r + step, n_row), c), device_id_type=MESH)

    def chain(src, send, recv, zs, lane, extra_source):
        def to(i, cc):
            return pltpu.make_async_remote_copy(
                src_ref=src, dst_ref=src, send_sem=send(i), recv_sem=recv,
                device_id=(r, cc), device_id_type=MESH)
        on_lane = core == lane
        up = on_lane & (z >= zs) & (z < n_z - 1)
        down = on_lane & (z <= zs) & (z > 0)
        others = ((0, up, jnp.minimum(c + 2, n_col - 1)), (1, down, jnp.maximum(c - 2, 0)),
                  (2, on_lane, z * 2 + 1 - core))

        def begin():
            @pl.when(jnp.logical_not(on_lane & (z == zs) & extra_source))
            def _():
                to(2, z * 2 + 1 - core).wait_recv()
            for i, cond, cc in others:
                @pl.when(cond)
                def _(i=i, cc=cc):
                    to(i, cc).start()

        def end():
            for i, cond, cc in others:
                @pl.when(cond)
                def _(i=i, cc=cc):
                    to(i, cc).wait_send()
        return begin, end

    ends = []

    def run_chain(*args):
        begin, end = chain(*args)
        begin()
        ends.append(end)

    def diag_chain(x):
        k, cc = owners[x]
        run_chain(diag.at[x], lambda i: d_csend.at[x, i], d_recv.at[x], 0, cc % 2, r == k)

    diag_chain(0)

    for k in range(2):
        @pl.when(r == k)
        def _(k=k):
            for step in range(1, n_row):
                strip_copy(k, step).start()

    piece = width // CHUNKS

    def panel_chain(k, q):
        for s in range(ratio):
            run_chain(brow.at[2 * s + k, pl.ds(q * piece, piece)],
                      lambda i, s=s: b_send.at[s, k, q, i], b_recv.at[s, k, q],
                      (r + n_row * s) // 2, lax.rem(r, 2), True)

    def need_strip(k):
        @pl.when(r != k)
        def _():
            strip_copy(k, 1).wait_recv()

    def keep_source(k):
        for s in range(ratio):
            @pl.when(c == r + n_row * s)
            def _(s=s):
                brow[2 * s + k] = bcol[k]

    def strip_tile(k, t):
        return jnp.concatenate(
            [strips[k, pl.ds(t * per + h, width, stride=tiles), :] for h in range(per)], axis=1)

    def finish(k):
        rr = lax.broadcasted_iota(jnp.int32, (width, width), 0)
        cc = lax.broadcasted_iota(jnp.int32, (width, width), 1)
        u_out[k] = jnp.where(cc >= rr, work[:, :width], 0.0)
        x_out[k] = jnp.where(cc <= rr, work[:, width:], 0.0)

    load_work(work, diag[0], width)
    for start in range(0, width, OUTER):
        eliminate_block(work, start, width)
        if start == 0:
            diag_chain(1)
        if start == OUTER:
            diag_chain(2)
    finish(0)
    b01 = dot(x_out[0], diag[1], ((1,), (0,)), HIGHEST).astype(jnp.bfloat16)
    b01_out[...] = b01
    need_strip(0)
    for t in range(col_blocks):
        bcol[0, :, t * width:(t + 1) * width] = dot(
            x_out[0], strip_tile(0, t), ((1,), (0,)), HIGHEST).astype(jnp.bfloat16)
    keep_source(0)
    load_work(work, diag[2] - dot(b01, b01, ((0,), (0,))), width)
    every = max(1, (width // OUTER) // CHUNKS)
    queue = list(range(CHUNKS))
    for start in range(0, width, OUTER):
        panel_chain(0, queue.pop(0))
        eliminate_block(work, start, width)
    for q in queue:
        panel_chain(0, q)
    finish(1)
    need_strip(1)
    for t in range(col_blocks):
        at = slice(t * width, (t + 1) * width)
        rest = strip_tile(1, t) - dot(b01_out[...], bcol[0, :, at], ((0,), (0,)))
        bcol[1, :, at] = dot(x_out[1], rest, ((1,), (0,)), HIGHEST).astype(jnp.bfloat16)
    keep_source(1)
    for q in range(CHUNKS):
        panel_chain(1, q)

    for end in ends:
        end()
    for x, (k, cc) in enumerate(owners):
        @pl.when((r == k) & (c == cc))
        def _(x=x):
            for step in range(1, n_row):
                diag_copy(x, step).wait_send()
    for k in range(2):
        @pl.when(r == k)
        def _(k=k):
            for step in range(1, n_row):
                strip_copy(k, step).wait_send()


def update_kernel(n_row, n_col, width, col_blocks, place, m_ref, brow, bcol, x_ref, u_ref, b01,
                  out_ref):
    rb = pl.program_id(0)
    r = place[0]
    c = place[1]
    tiles = col_blocks * width // 128
    per = width // 128
    left = brow[...].reshape(2 * width, width)
    right = bcol[...].reshape(2 * width, col_blocks * width)
    for t in range(col_blocks):
        new = dot(left, right[:, t * width:(t + 1) * width], ((0,), (0,)))
        for h in range(per):
            at = pl.ds(t * per + h, width, stride=tiles)
            out_ref[at, :] = m_ref[at, :] - new[:, h * 128:(h + 1) * 128]

    top = (rb == 0) & (r < 2)

    @pl.when(top)
    def _():
        out_ref[...] = jnp.zeros_like(out_ref)

    def put(block):
        for h in range(per):
            out_ref[pl.ds(h, width, stride=tiles), :] = block[:, h * 128:(h + 1) * 128]

    def get():
        return jnp.concatenate(
            [m_ref[pl.ds(h, width, stride=tiles), :] for h in range(per)], axis=1)

    @pl.when((c == 0) & jnp.logical_not((rb == 0) & (r == 0)))
    def _():
        put(dot(get(), x_ref[0], ((1,), (1,)), HIGHEST))

    @pl.when((c == 1) & jnp.logical_not(top))
    def _():
        rest = get() - dot(left[:width], b01[...], ((0,), (0,)))
        put(dot(rest, x_ref[1], ((1,), (1,)), HIGHEST))

    @pl.when((rb == 0) & (r == c) & (r < 2))
    def _():
        put(jnp.where(r == 0, u_ref[0], u_ref[1]).T)


def body(n_row, n_col, trailing):
    shape = trailing.shape
    row_blocks, width, col_blocks = shape[0], shape[2], shape[3]
    ratio = n_col // n_row
    tiles = col_blocks * width // 128
    block_rows = width * tiles
    local = trailing.reshape(row_blocks * block_rows, 128)
    wide = col_blocks * width
    vmem = pl.BlockSpec(memory_space=pltpu.VMEM)
    x_f, u_f, b01, bcol, brow = pl.pallas_call(
        functools.partial(panel_kernel, n_row, n_col, width, col_blocks),
        out_shape=(
            jax.ShapeDtypeStruct((2, width, width), jnp.float32),
            jax.ShapeDtypeStruct((2, width, width), jnp.float32),
            jax.ShapeDtypeStruct((width, width), jnp.bfloat16),
            jax.ShapeDtypeStruct((2, width, wide), jnp.bfloat16),
            jax.ShapeDtypeStruct((2 * ratio, width, wide), jnp.bfloat16),
        ),
        in_specs=[pl.BlockSpec(memory_space=pl.ANY)],
        out_specs=(vmem,) * 5,
        scratch_shapes=[
            pltpu.VMEM((2, block_rows, 128), jnp.float32),
            pltpu.VMEM((3, width, width), jnp.float32),
            pltpu.VMEM((width, 2 * width), jnp.float32),
            pltpu.SemaphoreType.DMA,
            pltpu.SemaphoreType.DMA((3, n_row - 1)),
            pltpu.SemaphoreType.DMA((3,)),
            pltpu.SemaphoreType.DMA((3, 3)),
            pltpu.SemaphoreType.DMA((2, n_row - 1)),
            pltpu.SemaphoreType.DMA((2,)),
            pltpu.SemaphoreType.DMA((ratio, 2, CHUNKS, 3)),
            pltpu.SemaphoreType.DMA((ratio, 2, CHUNKS)),
        ],
        compiler_params=pltpu.CompilerParams(
            collective_id=0, has_side_effects=True, vmem_limit_bytes=48 * 1024 * 1024),
        name="panels",
    )(local)
    place = jnp.stack([lax.axis_index("row"), lax.axis_index("col")]).astype(jnp.int32)
    out = pl.pallas_call(
        functools.partial(update_kernel, n_row, n_col, width, col_blocks),
        grid_spec=pltpu.PrefetchScalarGridSpec(
            num_scalar_prefetch=1,
            grid=(row_blocks,),
            in_specs=[
                pl.BlockSpec((block_rows, 128), lambda i, p: (i, 0)),
                pl.BlockSpec((2, width, width), lambda i, p: (i % ratio, 0, i // ratio)),
                pl.BlockSpec((2, width, wide), lambda i, p: (0, 0, 0)),
                pl.BlockSpec((2, width, width), lambda i, p: (0, 0, 0)),
                pl.BlockSpec((2, width, width), lambda i, p: (0, 0, 0)),
                pl.BlockSpec((width, width), lambda i, p: (0, 0)),
            ],
            out_specs=pl.BlockSpec((block_rows, 128), lambda i, p: (i, 0)),
        ),
        out_shape=jax.ShapeDtypeStruct(local.shape, jnp.float32),
        compiler_params=pltpu.CompilerParams(vmem_limit_bytes=48 * 1024 * 1024),
        name="update",
    )(place, local, brow, bcol, x_f, u_f, b01)
    return out.reshape(shape)


def solution(mesh):
    placed = P(None, "row", None, None, "col", None)
    return jax.shard_map(
        functools.partial(body, mesh.shape["row"], mesh.shape["col"]),
        mesh=mesh,
        in_specs=(placed,),
        out_specs=placed,
        check_vma=False,
    )
```

time: 628 us -> 252 us (0.40)
  the two profiles are of different devices: /device:TPU:0 before, /device:TPU:5 now
where the time goes in v1:
time: 252 us
  Pallas kernels  252 us (100%)
    pallas_call x1, Pallas kernels, body(): pl.pallas_call(functools.partial(panel_kernel, n_row, n_col, width, col_b...  235 us
    pallas_call x1, Pallas kernels, body(): pl.pallas_call(functools.partial(update_kernel, n_row, n_col, width, col_...  17 us

profile of v1, /device:TPU:5, one launch (start us, length us, event | category | flops | bytes accessed | tf_op | source)
XLA Modules:
  0.0 251.6 jit_solution(1570319858236549499)
XLA Ops:
  0.0 0.1 pad_add_fusion.place
  0.1 234.5 %panels.1 = (f32[2,256,256]{2,1,0:T(8,128)S(1)}, f32[2,256,256]{2,1,0:T(8,128)S(1)}, bf16[256,256]{1,0:T(8,128)(2,1)S(1)}, bf16[2,256,1280]{2,1,0:T(8,128)(2,1)S(1)}, bf16[4,256,1280]{2,1,0:T(8,128)(2,1)S(1)}) custom-call(f32[25600,128]{1,0:T(8,128)} %bitcast.4), custom_call_target="tpu_custom_call" | custom-call | tf_op jit(solution)/shard_map/panels/pallas_call | solution.py:299
  234.6 17.0 %update.1 = f32[25600,128]{1,0:T(8,128)} custom-call(s32[2]{0:T(128)S(1)} %pad_add_fusion.place, f32[25600,128]{1,0:T(8,128)} %bitcast.5, bf16[4,256,1280]{2,1,0:T(8,128)(2,1)S(1)} %get-tuple-element.10.brow, bf16[2,256,1280]{2,1,0:T(8,128)(2,1)S(1)} %get-tuple-element.11.bcol, f32[2,256,256]{2,1,0:T(8,128)S(1)} %get-tuple-element.12.x_ref, ...), custom_call_target="tpu_custom_call" | custom-call | tf_op jit(solution)/shard_map/update/pallas_call | solution.py:328

commit v2 on v1

--- a/solution.py
+++ b/solution.py
@@ -11,7 +11,7 @@
 HIGHEST = lax.Precision.HIGHEST
 OUTER = 64
 STRIP = 8
-CHUNKS = 4
+PARTS = 4
 
 
 def dot(a, b, dims, precision=None):
@@ -103,26 +103,61 @@
         own.wait()
 
     owners = ((0, 0), (0, 1), (1, 1))
-
-    def diag_copy(x, step):
+    part = width // PARTS
+    blocks = width // OUTER
+
+    def diag_piece(x, p):
+        return diag.at[x, pl.ds(p * part, part)]
+
+    def diag_copy(x, p, step):
         return pltpu.make_async_remote_copy(
-            src_ref=diag.at[x], dst_ref=diag.at[x], send_sem=d_send.at[x, step - 1],
-            recv_sem=d_recv.at[x], device_id=(lax.rem(r + step, n_row), c), device_id_type=MESH)
-
-    for x, (k, cc) in enumerate(owners):
+            src_ref=diag_piece(x, p), dst_ref=diag_piece(x, p),
+            send_sem=d_send.at[x, p, step - 1], recv_sem=d_recv.at[x, p],
+            device_id=(lax.rem(r + step, n_row), c), device_id_type=MESH)
+
+    def diag_start(x):
+        k, cc = owners[x]
+
         @pl.when((r == k) & (c == cc))
-        def _(x=x, k=k):
+        def _():
             for h in range(per):
                 diag[x, :, h * 128:(h + 1) * 128] = strips[k, pl.ds(h, width, stride=tiles), :]
-            for step in range(1, n_row):
-                diag_copy(x, step).start()
-
-    def strip_copy(k, step):
+            for p in range(PARTS):
+                for step in range(1, n_row):
+                    diag_copy(x, p, step).start()
+
+    half = strip_rows // PARTS
+    buddy = r + 1 - 2 * lax.rem(r, 2)
+
+    def strip_copy(k, p, i, target):
+        piece = strips.at[k, pl.ds(p * half, half)]
         return pltpu.make_async_remote_copy(
-            src_ref=strips.at[k], dst_ref=strips.at[k], send_sem=s_send.at[k, step - 1],
-            recv_sem=s_recv.at[k], device_id=(lax.rem(r + step, n_row), c), device_id_type=MESH)
-
-    def chain(src, send, recv, zs, lane, extra_source):
+            src_ref=piece, dst_ref=piece, send_sem=s_send.at[k, p, i],
+            recv_sem=s_recv.at[k, p], device_id=(target, c), device_id_type=MESH)
+
+    def strip_start():
+        for k in range(2):
+            @pl.when(r == k)
+            def _(k=k):
+                for p in range(PARTS):
+                    for i in range(1, n_row // 2):
+                        strip_copy(k, p, i, k + 2 * i).start()
+                    strip_copy(k, p, 0, buddy).start()
+
+    def strip_relay(p):
+        for k in range(2):
+            @pl.when((r != k) & (lax.rem(r, 2) == k))
+            def _(k=k):
+                strip_copy(k, p, 0, buddy).wait_recv()
+                strip_copy(k, p, 0, buddy).start()
+
+    def strip_need(k):
+        @pl.when(lax.rem(r, 2) != k)
+        def _():
+            for p in range(PARTS):
+                strip_copy(k, p, 0, buddy).wait_recv()
+
+    def chain(src, send, recv, zs, lane):
         def to(i, cc):
             return pltpu.make_async_remote_copy(
                 src_ref=src, dst_ref=src, send_sem=send(i), recv_sem=recv,
@@ -130,62 +165,63 @@
         on_lane = core == lane
         up = on_lane & (z >= zs) & (z < n_z - 1)
         down = on_lane & (z <= zs) & (z > 0)
-        others = ((0, up, jnp.minimum(c + 2, n_col - 1)), (1, down, jnp.maximum(c - 2, 0)),
-                  (2, on_lane, z * 2 + 1 - core))
-
-        def begin():
-            @pl.when(jnp.logical_not(on_lane & (z == zs) & extra_source))
-            def _():
-                to(2, z * 2 + 1 - core).wait_recv()
-            for i, cond, cc in others:
+        links = ((0, up, jnp.minimum(c + 2, n_col - 1)), (1, down, jnp.maximum(c - 2, 0)),
+                 (2, on_lane, z * 2 + 1 - core))
+
+        def receive():
+            to(2, z * 2 + 1 - core).wait_recv()
+
+        def send_on():
+            for i, cond, cc in links:
                 @pl.when(cond)
                 def _(i=i, cc=cc):
                     to(i, cc).start()
 
         def end():
-            for i, cond, cc in others:
+            for i, cond, cc in links:
                 @pl.when(cond)
                 def _(i=i, cc=cc):
                     to(i, cc).wait_send()
-        return begin, end
-
-    ends = []
-
-    def run_chain(*args):
-        begin, end = chain(*args)
-        begin()
-        ends.append(end)
+        return receive, send_on, end
+
+    def diag_link(x, p):
+        return chain(diag_piece(x, p), lambda i: d_csend.at[x, p, i], d_recv.at[x, p], 0,
+                     owners[x][1] % 2)
 
     def diag_chain(x):
         k, cc = owners[x]
-        run_chain(diag.at[x], lambda i: d_csend.at[x, i], d_recv.at[x], 0, cc % 2, r == k)
-
-    diag_chain(0)
-
-    for k in range(2):
-        @pl.when(r == k)
-        def _(k=k):
-            for step in range(1, n_row):
-                strip_copy(k, step).start()
-
-    piece = width // CHUNKS
-
-    def panel_chain(k, q):
-        for s in range(ratio):
-            run_chain(brow.at[2 * s + k, pl.ds(q * piece, piece)],
-                      lambda i, s=s: b_send.at[s, k, q, i], b_recv.at[s, k, q],
-                      (r + n_row * s) // 2, lax.rem(r, 2), True)
-
-    def need_strip(k):
-        @pl.when(r != k)
-        def _():
-            strip_copy(k, 1).wait_recv()
-
-    def keep_source(k):
+        for p in range(PARTS):
+            receive, send_on, _ = diag_link(x, p)
+
+            @pl.when(jnp.logical_not((r == k) & (c == cc)))
+            def _(receive=receive):
+                receive()
+            send_on()
+
+    def panel_link(s, k, t):
+        return chain(brow.at[2 * s + k, :, pl.ds(t * width, width)],
+                     lambda i: b_send.at[s, k, t, i], b_recv.at[s, k, t],
+                     (r + n_row * s) // 2, lax.rem(r, 2))
+
+    lane_core = core == lax.rem(r, 2)
+
+    def distance(s):
+        return jnp.abs(z - (r + n_row * s) // 2)
+
+    def panel_source(k, t):
         for s in range(ratio):
             @pl.when(c == r + n_row * s)
             def _(s=s):
-                brow[2 * s + k] = bcol[k]
+                at = slice(t * width, (t + 1) * width)
+                brow[2 * s + k, :, at] = bcol[k, :, at]
+                panel_link(s, k, t)[1]()
+
+    def panel_relay(k, t, s, cond):
+        @pl.when(cond)
+        def _():
+            receive, send_on, _ = panel_link(s, k, t)
+            receive()
+            send_on()
 
     def strip_tile(k, t):
         return jnp.concatenate(
@@ -197,51 +233,82 @@
         u_out[k] = jnp.where(cc >= rr, work[:, :width], 0.0)
         x_out[k] = jnp.where(cc <= rr, work[:, width:], 0.0)
 
+    diag_start(0)
+
+    @pl.when(z > 0)
+    def _():
+        strip_start()
+
+    diag_chain(0)
     load_work(work, diag[0], width)
-    for start in range(0, width, OUTER):
-        eliminate_block(work, start, width)
-        if start == 0:
+    for b in range(blocks):
+        eliminate_block(work, b * OUTER, width)
+        if b == 0:
+            diag_start(1)
+            diag_start(2)
+
+            @pl.when(z == 0)
+            def _():
+                strip_start()
+        if b == 1:
+            strip_relay(0)
+        if b == 2:
+            strip_relay(1)
             diag_chain(1)
-        if start == OUTER:
+        if b == 3:
+            strip_relay(2)
             diag_chain(2)
     finish(0)
     b01 = dot(x_out[0], diag[1], ((1,), (0,)), HIGHEST).astype(jnp.bfloat16)
     b01_out[...] = b01
-    need_strip(0)
+    strip_relay(3)
+    strip_need(0)
     for t in range(col_blocks):
         bcol[0, :, t * width:(t + 1) * width] = dot(
             x_out[0], strip_tile(0, t), ((1,), (0,)), HIGHEST).astype(jnp.bfloat16)
-    keep_source(0)
+        panel_source(0, t)
     load_work(work, diag[2] - dot(b01, b01, ((0,), (0,))), width)
-    every = max(1, (width // OUTER) // CHUNKS)
-    queue = list(range(CHUNKS))
-    for start in range(0, width, OUTER):
-        panel_chain(0, queue.pop(0))
-        eliminate_block(work, start, width)
-    for q in queue:
-        panel_chain(0, q)
+    for b in range(blocks):
+        eliminate_block(work, b * OUTER, width)
+        for s in range(ratio):
+            far = distance(s) >= b + 1 if b == blocks - 1 else distance(s) == b + 1
+            for t in range(col_blocks):
+                panel_relay(0, t, s, lane_core & far)
     finish(1)
-    need_strip(1)
+    strip_need(1)
     for t in range(col_blocks):
         at = slice(t * width, (t + 1) * width)
         rest = strip_tile(1, t) - dot(b01_out[...], bcol[0, :, at], ((0,), (0,)))
         bcol[1, :, at] = dot(x_out[1], rest, ((1,), (0,)), HIGHEST).astype(jnp.bfloat16)
-    keep_source(1)
-    for q in range(CHUNKS):
-        panel_chain(1, q)
-
-    for end in ends:
-        end()
+        panel_source(1, t)
+    for t in range(col_blocks):
+        for s in range(ratio):
+            panel_relay(0, t, s, jnp.logical_not(lane_core))
+            panel_relay(1, t, s, jnp.logical_not(lane_core & (distance(s) == 0)))
+
     for x, (k, cc) in enumerate(owners):
-        @pl.when((r == k) & (c == cc))
-        def _(x=x):
-            for step in range(1, n_row):
-                diag_copy(x, step).wait_send()
+        for p in range(PARTS):
+            diag_link(x, p)[2]()
+
+            @pl.when((r == k) & (c == cc))
+            def _(x=x, p=p):
+                for step in range(1, n_row):
+                    diag_copy(x, p, step).wait_send()
     for k in range(2):
+        @pl.when(lax.rem(r, 2) == k)
+        def _(k=k):
+            for p in range(PARTS):
+                strip_copy(k, p, 0, buddy).wait_send()
+
         @pl.when(r == k)
         def _(k=k):
-            for step in range(1, n_row):
-                strip_copy(k, step).wait_send()
+            for p in range(PARTS):
+                for i in range(1, n_row // 2):
+                    strip_copy(k, p, i, k + 2 * i).wait_send()
+    for s in range(ratio):
+        for k in range(2):
+            for t in range(col_blocks):
+                panel_link(s, k, t)[2]()
 
 
 def update_kernel(n_row, n_col, width, col_blocks, place, m_ref, brow, bcol, x_ref, u_ref, b01,
@@ -312,13 +379,13 @@
             pltpu.VMEM((3, width, width), jnp.float32),
             pltpu.VMEM((width, 2 * width), jnp.float32),
             pltpu.SemaphoreType.DMA,
-            pltpu.SemaphoreType.DMA((3, n_row - 1)),
-            pltpu.SemaphoreType.DMA((3,)),
-            pltpu.SemaphoreType.DMA((3, 3)),
-            pltpu.SemaphoreType.DMA((2, n_row - 1)),
-            pltpu.SemaphoreType.DMA((2,)),
-            pltpu.SemaphoreType.DMA((ratio, 2, CHUNKS, 3)),
-            pltpu.SemaphoreType.DMA((ratio, 2, CHUNKS)),
+            pltpu.SemaphoreType.DMA((3, PARTS, n_row - 1)),
+            pltpu.SemaphoreType.DMA((3, PARTS)),
+            pltpu.SemaphoreType.DMA((3, PARTS, 3)),
+            pltpu.SemaphoreType.DMA((2, PARTS, n_row // 2)),
+            pltpu.SemaphoreType.DMA((2, PARTS)),
+            pltpu.SemaphoreType.DMA((ratio, 2, col_blocks, 3)),
+            pltpu.SemaphoreType.DMA((ratio, 2, col_blocks)),
         ],
         compiler_params=pltpu.CompilerParams(
             collective_id=0, has_side_effects=True, vmem_limit_bytes=48 * 1024 * 1024),

time: 252 us -> 121 us (0.48)
  the two profiles are of different devices: /device:TPU:5 before, /device:TPU:7 now
where the time goes in v2:
time: 121 us
  Pallas kernels  121 us (100%)
    pallas_call x1, Pallas kernels, body(): pl.pallas_call(functools.partial(panel_kernel, n_row, n_col, width, col_b...  104 us
    pallas_call x1, Pallas kernels, body(): pl.pallas_call(functools.partial(update_kernel, n_row, n_col, width, col_...  17 us

profile of v2, /device:TPU:7, one launch (start us, length us, event | category | flops | bytes accessed | tf_op | source)
XLA Modules:
  0.0 121.0 jit_solution(2653191859304487224)
XLA Ops:
  0.0 0.1 pad_add_fusion.place
  0.1 103.9 %panels.1 = (f32[2,256,256]{2,1,0:T(8,128)S(1)}, f32[2,256,256]{2,1,0:T(8,128)S(1)}, bf16[256,256]{1,0:T(8,128)(2,1)S(1)}, bf16[2,256,1280]{2,1,0:T(8,128)(2,1)S(1)}, bf16[4,256,1280]{2,1,0:T(8,128)(2,1)S(1)}) custom-call(f32[25600,128]{1,0:T(8,128)} %bitcast.4), custom_call_target="tpu_custom_call" | custom-call | tf_op jit(solution)/shard_map/panels/pallas_call | solution.py:366
  103.9 17.0 %update.1 = f32[25600,128]{1,0:T(8,128)} custom-call(s32[2]{0:T(128)S(1)} %pad_add_fusion.place, f32[25600,128]{1,0:T(8,128)} %bitcast.5, bf16[4,256,1280]{2,1,0:T(8,128)(2,1)S(1)} %get-tuple-element.10.brow, bf16[2,256,1280]{2,1,0:T(8,128)(2,1)S(1)} %get-tuple-element.11.bcol, f32[2,256,256]{2,1,0:T(8,128)S(1)} %get-tuple-element.12.x_ref, ...), custom_call_target="tpu_custom_call" | custom-call | tf_op jit(solution)/shard_map/update/pallas_call | solution.py:395

commit v3 on v2

--- a/solution.py
+++ b/solution.py
@@ -21,12 +21,15 @@
 
 
 def eliminate_block(work, start, width):
+    stop = start + OUTER
     tile = (start // 128) * 128
+    edge = width + -(-stop // 128) * 128
+    first = start - tile
 
     def strip(s, carry):
         j0 = pl.multiple_of(start + s * STRIP, STRIP)
-        rows = work[pl.ds(j0, STRIP), :]
-        near = rows[:, tile:tile + 128]
+        rows = work[pl.ds(j0, STRIP), tile:edge]
+        near = rows[:, :128]
         lane = lax.broadcasted_iota(jnp.int32, (STRIP, 128), 1) + tile
         sub = lax.broadcasted_iota(jnp.int32, (STRIP, 1), 0)
         cols = [
@@ -42,17 +45,16 @@
                 cols[m] = cols[m] - mult * mult[m:m + 1]
             row = rows[k:k + 1] * inv
             rows = jnp.where(sub == k, row, jnp.where(sub > k, rows - mult * row, rows))
-        work[pl.ds(j0, STRIP), :] = rows
+        work[pl.ds(j0, STRIP), tile:edge] = rows
         here = lax.broadcasted_iota(jnp.int32, (STRIP, OUTER), 1)
-        left = jnp.where(here >= (s + 1) * STRIP, rows[:, start:start + OUTER], 0.0)
-        work[start:start + OUTER, :] -= dot(left, rows, ((0,), (0,)), HIGHEST)
+        left = jnp.where(here >= (s + 1) * STRIP, rows[:, first:first + OUTER], 0.0)
+        work[start:stop, tile:edge] -= dot(left, rows, ((0,), (0,)), HIGHEST)
         return carry
 
     lax.fori_loop(0, OUTER // STRIP, strip, 0)
-    stop = start + OUTER
     if stop < width:
-        done = work[start:stop, :]
-        work[stop:width, :] -= dot(done[:, stop:width], done, ((0,), (0,)), HIGHEST)
+        done = work[start:stop, tile:edge]
+        work[stop:width, tile:edge] -= dot(done[:, stop - tile:width - tile], done, ((0,), (0,)), HIGHEST)
 
 
 def load_work(work, block, width):
@@ -261,19 +263,21 @@
     finish(0)
     b01 = dot(x_out[0], diag[1], ((1,), (0,)), HIGHEST).astype(jnp.bfloat16)
     b01_out[...] = b01
-    strip_relay(3)
-    strip_need(0)
-    for t in range(col_blocks):
-        bcol[0, :, t * width:(t + 1) * width] = dot(
-            x_out[0], strip_tile(0, t), ((1,), (0,)), HIGHEST).astype(jnp.bfloat16)
-        panel_source(0, t)
     load_work(work, diag[2] - dot(b01, b01, ((0,), (0,))), width)
     for b in range(blocks):
         eliminate_block(work, b * OUTER, width)
-        for s in range(ratio):
-            far = distance(s) >= b + 1 if b == blocks - 1 else distance(s) == b + 1
+        if b == 0:
+            strip_relay(3)
+        if b == 1:
+            strip_need(0)
             for t in range(col_blocks):
-                panel_relay(0, t, s, lane_core & far)
+                bcol[0, :, t * width:(t + 1) * width] = dot(
+                    x_out[0], strip_tile(0, t), ((1,), (0,)), HIGHEST).astype(jnp.bfloat16)
+                panel_source(0, t)
+        if b >= 2:
+            for s in range(ratio):
+                for t in range(col_blocks):
+                    panel_relay(0, t, s, lane_core & (distance(s) == b - 1))
     finish(1)
     strip_need(1)
     for t in range(col_blocks):
@@ -283,7 +287,7 @@
         panel_source(1, t)
     for t in range(col_blocks):
         for s in range(ratio):
-            panel_relay(0, t, s, jnp.logical_not(lane_core))
+            panel_relay(0, t, s, jnp.logical_not(lane_core & (distance(s) <= blocks - 2)))
             panel_relay(1, t, s, jnp.logical_not(lane_core & (distance(s) == 0)))
 
     for x, (k, cc) in enumerate(owners):

time: 121 us -> 115 us (0.950)
  Pallas kernels: 121 us -> 115 us
    pallas_call x1, Pallas kernels: 104 us -> 97.7 us  [body(): pl.pallas_call(functools.partial(panel_kernel, n_row, n_col, width, col_b...]
where the time goes in v3:
time: 115 us
  Pallas kernels  115 us (100%)
    pallas_call x1, Pallas kernels, body(): pl.pallas_call(functools.partial(panel_kernel, n_row, n_col, width, col_b...  97.7 us
    pallas_call x1, Pallas kernels, body(): pl.pallas_call(functools.partial(update_kernel, n_row, n_col, width, col_...  17 us

profile of v3, /device:TPU:7, one launch (start us, length us, event | category | flops | bytes accessed | tf_op | source)
XLA Modules:
  0.0 114.8 jit_solution(6969531254534123135)
XLA Ops:
  0.0 0.1 pad_add_fusion.place
  0.1 97.7 %panels.1 = (f32[2,256,256]{2,1,0:T(8,128)S(1)}, f32[2,256,256]{2,1,0:T(8,128)S(1)}, bf16[256,256]{1,0:T(8,128)(2,1)S(1)}, bf16[2,256,1280]{2,1,0:T(8,128)(2,1)S(1)}, bf16[4,256,1280]{2,1,0:T(8,128)(2,1)S(1)}) custom-call(f32[25600,128]{1,0:T(8,128)} %bitcast.4), custom_call_target="tpu_custom_call" | custom-call | tf_op jit(solution)/shard_map/panels/pallas_call | solution.py:370
  97.8 17.0 %update.1 = f32[25600,128]{1,0:T(8,128)} custom-call(s32[2]{0:T(128)S(1)} %pad_add_fusion.place, f32[25600,128]{1,0:T(8,128)} %bitcast.5, bf16[4,256,1280]{2,1,0:T(8,128)(2,1)S(1)} %get-tuple-element.10.brow, bf16[2,256,1280]{2,1,0:T(8,128)(2,1)S(1)} %get-tuple-element.11.bcol, f32[2,256,256]{2,1,0:T(8,128)S(1)} %get-tuple-element.12.x_ref, ...), custom_call_target="tpu_custom_call" | custom-call | tf_op jit(solution)/shard_map/update/pallas_call | solution.py:399
